TPU v7x, 32 devices: a whole 2x2x4 slice. The times are simulated.
32 devices in a mesh: tile: 8 (over z, x), wp: 4 (over y, core).
Axes of the slice: x: 2, y: 2, z: 4, core: 2. Of those that a mesh axis runs over, the one named last changes fastest.
Arguments:
- visibilities: float32 [8192, 2, 128], P(('tile', 'wp')), may hold values from -6 to 6
- vis_weight: float32 [8192, 128], P(('tile', 'wp')), may hold values from 0.2 to 5
- cell_index: int32 [8192, 128], P(('tile', 'wp')), may hold values from 0 to 4095
- tap_offsets: int32 [8192, 128], P(('tile', 'wp')), may hold values from 0 to 255
- routes: int32 [8192, 1], P(('tile', 'wp')), may hold values from 0 to 31; in each aligned block of 256 rows (0 to 255, 256 to 511, ...) at most 16 rows name the same one
- patch_index: int32 [8192], P(('tile', 'wp')), may hold values from 0 to 255
- kernel: float32 [16, 8], replicated, may hold values from 0.1 to 1
Outputs:
- uv_grid: float32 [4, 8, 2, 1024, 1024], P('wp', 'tile')
Inputs may be any that keep to these rules, and one draw needn't show every extreme that they name: `routes`: the 256 blocks of one device name no value more than 16 times, a bound that some block reaches.
All inputs are finite; a program needn't handle non-finite values.
Results may differ from a plain program's by a relative error of at most 0.0003.
Values sent between devices are 32-bit elements; how exact they have to be, the bound alone decides.
No kernel may reach another device: no remote copies, remote signals or barrier semaphores. Data moves between devices by JAX's collectives and lax.ppermute only.
A program may use at most 192 MiB of HBM per device.

v0:
```python
import functools

import jax
import jax.numpy as jnp
from jax import lax
from jax.experimental import pallas as pl
from jax.experimental.pallas import tpu as pltpu
from jax.sharding import PartitionSpec as P

TCOLS = 8
SUB = 64
KW = 8
OVER = 16
TILE = 1024
ROWS = 128
SIDE = TILE // SUB
PATCHES = SIDE * SIDE
ROW_BLOCK = 2 * (SUB + KW)
FIRST = SIDE
DUMMY = FIRST + PATCHES
LONG, SHORT = 64, 16

f32 = jnp.float32
bf16 = jnp.bfloat16


def lanes(shape):
    return lax.broadcasted_iota(jnp.int32, shape, len(shape) - 1)


def pack_kernel(peers, cap, routes, patch, vis, weight, cell, tap, out, acc, *scratch):
    routes_s, patch_s, vis_v, weight_v, cell_v, tap_v, meta, meta_v, place, sems = scratch
    blocks = vis.shape[0]
    rows = 3 * cap + 1
    sources = (routes, patch, vis, weight, cell, tap)
    targets = (routes_s, patch_s, vis_v, weight_v, cell_v, tap_v)
    copies = [pltpu.make_async_copy(a, b, sems.at[i]) for i, (a, b) in enumerate(zip(sources, targets))]
    for copy in copies:
        copy.start()

    steps = blocks // 8
    early = acc.shape[0] - 6 * steps

    def clear_accumulators(first, number):
        for i in range(number):
            acc[first + i] = jnp.zeros((ROW_BLOCK, ROWS), f32)

    def clear(d, carry):
        meta[d, cap] = 0
        return carry

    def clear_one(i, carry):
        clear_accumulators(i, 1)
        return carry

    lax.fori_loop(0, peers, clear, 0, unroll=8)
    lax.fori_loop(0, early, clear_one, 0)
    copies[0].wait()
    copies[1].wait()

    def choose(step, carry):
        clear_accumulators(early + 4 * step, 4)
        for i in range(8):
            b = step * 8 + i
            d = routes_s[b]
            k = meta[d, cap]
            meta[d, cap] = k + 1
            meta[d, k] = patch_s[b]
            place[b] = d * rows + 3 * k
        return carry

    lax.fori_loop(0, steps, choose, 0)
    meta_copy = pltpu.make_async_copy(meta, meta_v, sems.at[6])
    meta_copy.start()
    for copy in copies[2:]:
        copy.wait()

    def move(step, carry):
        clear_accumulators(early + 4 * steps + 2 * step, 2)
        first = pl.multiple_of(step * 8, 8)
        block_rows = pl.ds(first, 8)
        w = weight_v[block_rows, :]
        c = cell_v[block_rows, :]
        t = tap_v[block_rows, :]
        at_u = ((t >> 4) << 3) | ((c >> 6) & 7)
        at_v = ((t & 15) << 3) | (c & 7)
        code = (((c >> 9) << 17) | (((c >> 3) & 7) << 14) | (at_u << 7) | at_v).astype(f32)
        for i in range(8):
            row = place[first + i]
            both = vis_v[first + i] * w[i : i + 1, :]
            out[row] = both[0:1, :]
            out[row + 1] = both[1:2, :]
            out[row + 2] = code[i : i + 1, :]
        return carry

    lax.fori_loop(0, steps, move, 0)
    meta_copy.wait()

    def put_meta(d, carry):
        out[d * rows + 3 * cap] = meta_v[pl.ds(d, 1), :].astype(f32)
        return carry

    lax.fori_loop(0, peers, put_meta, 0, unroll=8)


def split(x):
    hi = x.astype(bf16)
    return hi, (x - hi.astype(f32)).astype(bf16)


def twice(x):
    return jnp.concatenate([x, x], axis=0)


def look_up(table, index):
    numbers = lax.GatherDimensionNumbers(
        offset_dims=(),
        collapsed_slice_dims=(1,),
        start_index_map=(1,),
        operand_batching_dims=(0,),
        start_indices_batching_dims=(0,),
    )
    return lax.gather(
        table, index[..., None], numbers, (1, 1), mode=lax.GatherScatterMode.PROMISE_IN_BOUNDS
    )


def spread(picks, values):
    zero = jnp.zeros((16, ROWS), bf16)
    return [[jnp.where(pick, value, zero) for pick in picks] for value in values]


def patch_product(re, im, code, parity, table, wide):
    sub = lax.broadcasted_iota(jnp.int32, (8, ROWS), 0)
    at_v = code & 127
    at_u = (code >> 7) & 127
    ku = look_up(table, at_u)
    kv = look_up(table, at_v)
    group_u = ((code >> 17) & 7) + jnp.where(sub < (at_u & 7), 1, 0)
    group_v = ((code >> 14) & 7) + jnp.where(sub < (at_v & 7), 1, 0) + 8 * parity
    step_u = twice(group_u.astype(f32)).astype(bf16)
    step_v = jnp.concatenate([group_v & 15, (group_v + 15) & 15], axis=0).astype(f32).astype(bf16)

    u_hi, u_lo = split(jnp.concatenate([re * ku, im * ku], axis=0))
    hi_rows, lo_rows = spread([step_u == float(g) for g in range(SUB // 8 + 1)], [u_hi, u_lo])
    left_hi, left_lo = jnp.concatenate(hi_rows, axis=0), jnp.concatenate(lo_rows, axis=0)
    v_hi, v_lo = split(twice(kv))
    hi_rows, lo_rows = spread([step_v == 2.0 * g for g in range(ROWS // 16)], [v_hi, v_lo])
    right_hi, right_lo = jnp.concatenate(hi_rows, axis=0), jnp.concatenate(lo_rows, axis=0)

    if wide:
        left = jnp.concatenate([left_hi, left_lo], axis=1)
        right = jnp.concatenate([right_hi, right_lo], axis=0)
        right = jnp.concatenate([right, right], axis=1)
    else:
        left = jnp.concatenate([left_hi, left_lo], axis=0)
        left = jnp.concatenate([left, left], axis=1)
        right = jnp.concatenate([right_hi, right_lo], axis=1)
    product = lax.dot_general(left, right, (((1,), (1,)), ((), ())), preferred_element_type=f32)
    if wide:
        return product[:, :ROWS] + product[:, ROWS:]
    return product[:ROW_BLOCK] + product[ROW_BLOCK:]


def tap_table(kernel):
    sub = lax.broadcasted_iota(jnp.int32, (8, ROWS), 0)
    lane = lanes((8, ROWS))
    which_tap = (sub - lane) & 7
    which_level = lane >> 3
    table = jnp.zeros((8, ROWS), f32)
    for a in range(KW):
        row = jnp.zeros((8, ROWS), f32)
        for o in range(OVER):
            row = jnp.where(which_level == o, kernel[a, o], row)
        table = jnp.where(which_tap == a, row, table)
    return table


def add_kernel(peers, cap, kernel, arrived, acc_in, acc, right, *scratch):
    meta_v, meta, slots, kernel_s, meta_sem, kernel_sem = scratch
    rows = 3 * cap + 1
    kernel_copy = pltpu.make_async_copy(kernel, kernel_s, kernel_sem)
    kernel_copy.start()
    lane_row = lanes((1, ROWS))

    def entries(s, carry):
        row = arrived[s * rows + 3 * cap].astype(jnp.int32)
        entry = (s * rows + 3 * lane_row) * 512 + (row + FIRST)
        meta_v[pl.ds(s, 1), :] = jnp.where(lane_row < cap, entry, row)
        return carry

    lax.fori_loop(0, peers, entries, 0, unroll=8)
    meta_copy = pltpu.make_async_copy(meta_v, meta, meta_sem)
    meta_copy.start()
    kernel_copy.wait()
    table = tap_table(kernel_s)
    meta_copy.wait()

    def gather_source(s, total):
        for k in range(cap):
            slots[total + k] = meta[s, k]
        return total + meta[s, cap]

    total = lax.fori_loop(0, peers, gather_source, 0, unroll=2)
    for k in range(SHORT):
        slots[total + k] = DUMMY

    def add(first, number):
        for i in range(number):
            entry = slots[first + i]
            row = entry >> 9
            where_to = entry & 511
            re = jnp.broadcast_to(arrived[row], (8, ROWS))
            im = jnp.broadcast_to(arrived[row + 1], (8, ROWS))
            code = jnp.broadcast_to(arrived[row + 2], (8, ROWS)).astype(jnp.int32)
            acc[where_to] += patch_product(re, im, code, entry & 1, table, i % 4 < 2)

    def long_step(step, carry):
        add(step * LONG, LONG)
        return carry

    long_steps = total // LONG
    lax.fori_loop(0, long_steps, long_step, 0)
    done = long_steps * LONG

    def short_step(step, carry):
        add(done + step * SHORT, SHORT)
        return carry

    lax.fori_loop(0, (total - done + SHORT - 1) // SHORT, short_step, 0)

    lane = lanes((8, ROWS))

    def pack_edge(pair, carry):
        for c in range(2):
            edge = jnp.zeros((8, ROWS), f32)
            for k in range(16):
                last = rows_of(acc, c, k % 8, pair * 2 + k // 8, SIDE - 1)
                moved = pltpu.roll(last, 8 * k, 1) if k else last
                edge = jnp.where((lane >> 3) == k, moved, edge)
            right[c, pair] = edge
        return carry

    lax.fori_loop(0, SIDE // 2, pack_edge, 0)


def rows_of(acc, c, h, band, col):
    part = acc[FIRST + band * SIDE + col, pl.ds(16 * h + 8 * c, 8), :]
    if h == 0:
        part = part + acc[band * SIDE + col, pl.ds(2 * SUB + 8 * c, 8), :]
    return part


def fold_kernel(with_low, acc, out, first, *rest):
    low, rest = (rest[0], rest[1:]) if with_low else (None, rest)
    stage, out_sems = rest
    lane = lanes((8, ROWS))

    def copy_out(band):
        rows = pl.ds(band * SUB, SUB)
        return pltpu.make_async_copy(
            stage.at[:, rows, :], out.at[:, rows, pl.ds(ROWS, TILE - ROWS)], out_sems.at[band]
        )

    def fold(band, carry):
        for c in range(2):
            for h in range(8):
                before = jnp.zeros((8, ROWS), f32)
                for t in range(TILE // ROWS):
                    even = rows_of(acc, c, h, band, 2 * t)
                    odd = rows_of(acc, c, h, band, 2 * t + 1)
                    rows = pl.ds(band * SUB + 8 * h, 8)
                    columns = even + jnp.where(lane < SUB, before, odd)
                    if t == 0:
                        first[c, rows, :] = columns
                    else:
                        stage[c, rows, pl.ds((t - 1) * ROWS, ROWS)] = columns
                    before = odd
        copy_out(band).start()
        return carry

    lax.fori_loop(0, SIDE, fold, 0)
    if with_low:
        for c in range(2):
            before = jnp.zeros((8, ROWS), f32)
            for t in range(TILE // ROWS):
                rows = pl.ds(2 * SUB + 8 * c, 8)
                even = acc[FIRST + (SIDE - 1) * SIDE + 2 * t, rows, :]
                odd = acc[FIRST + (SIDE - 1) * SIDE + 2 * t + 1, rows, :]
                low[c, :, pl.ds(t * ROWS, ROWS)] = even + jnp.where(lane < SUB, before, odd)
                before = odd
            low[c, :, pl.ds(TILE, ROWS)] = jnp.where(lane < KW, before, 0.0)

    def finish(band, carry):
        copy_out(band).wait()
        return carry

    lax.fori_loop(0, SIDE, finish, 0)


def edge_kernel(edge, first, grid_in, grid_out, columns, out_sems):
    lane = lanes((8, ROWS))
    pairs = SIDE // 2

    def put(pair):
        rows = pl.ds(pair * 2 * SUB, 2 * SUB)
        return pltpu.make_async_copy(
            columns.at[:, rows, :], grid_out.at[:, rows, pl.ds(0, ROWS)], out_sems.at[pair]
        )

    def add(pair, carry):
        for c in range(2):
            packed = edge[c, pair]
            for k in range(16):
                moved = pltpu.roll(packed, ROWS - 8 * k, 1) if k else packed
                rows = pl.ds(pair * 2 * SUB + 8 * k, 8)
                columns[c, rows, :] = first[c, rows, :] + jnp.where(lane < KW, moved, 0.0)
        put(pair).start()
        return carry

    lax.fori_loop(0, pairs, add, 0)
    for pair in range(pairs):
        put(pair).wait()


def in_hbm(x):
    return pltpu.with_memory_space_constraint(x, pltpu.HBM)


def shifted(block, axis, distance):
    devices = range(lax.axis_size(axis))
    route = [(i - distance, i) for i in devices if i - distance in devices]
    return lax.ppermute(block, axis, route)


def shards(visibilities, vis_weight, cell_index, tap_offsets, routes, patch_index, kernel):
    blocks = visibilities.shape[0]
    tile_count = lax.axis_size("tile")
    plane_count = lax.axis_size("wp")
    peers = tile_count * plane_count
    cap = max(2, 2 * blocks // peers)
    rows = 3 * cap + 1
    vmem = pl.BlockSpec(memory_space=pltpu.VMEM)
    hbm = pl.BlockSpec(memory_space=pltpu.HBM)

    acc_shape = (max(DUMMY + 1, 6 * (blocks // 8)), ROW_BLOCK, ROWS)

    buckets, acc = pl.pallas_call(
        functools.partial(pack_kernel, peers, cap),
        out_shape=[jax.ShapeDtypeStruct((peers * rows, 1, ROWS), f32), pltpu.VMEM(acc_shape, f32)],
        in_specs=[hbm] * 6,
        out_specs=[vmem, vmem],
        scratch_shapes=[
            pltpu.SMEM((blocks,), jnp.int32),
            pltpu.SMEM((blocks,), jnp.int32),
            pltpu.VMEM((blocks, 2, ROWS), f32),
            pltpu.VMEM((blocks, ROWS), f32),
            pltpu.VMEM((blocks, ROWS), jnp.int32),
            pltpu.VMEM((blocks, ROWS), jnp.int32),
            pltpu.SMEM((peers, ROWS), jnp.int32),
            pltpu.VMEM((peers, ROWS), jnp.int32),
            pltpu.SMEM((blocks,), jnp.int32),
            pltpu.SemaphoreType.DMA((7,)),
        ],
        compiler_params=pltpu.CompilerParams(vmem_limit_bytes=8 << 20),
        name="pack",
    )(*[in_hbm(x) for x in (routes[:, 0], patch_index, visibilities, vis_weight, cell_index, tap_offsets)])

    arrived = lax.all_to_all(buckets, ("tile", "wp"), split_axis=0, concat_axis=0, tiled=True)

    acc, right = pl.pallas_call(
        functools.partial(add_kernel, peers, cap),
        out_shape=[pltpu.VMEM(acc_shape, f32), jax.ShapeDtypeStruct((2, SIDE // 2, 8, ROWS), f32)],
        in_specs=[hbm, vmem, vmem],
        out_specs=[vmem, vmem],
        scratch_shapes=[
            pltpu.VMEM((peers, ROWS), jnp.int32),
            pltpu.SMEM((peers, ROWS), jnp.int32),
            pltpu.SMEM((peers * cap + max(cap, SHORT),), jnp.int32),
            pltpu.SMEM((KW, OVER), f32),
            pltpu.SemaphoreType.DMA,
            pltpu.SemaphoreType.DMA,
        ],
        input_output_aliases={2: 0},
        compiler_params=pltpu.CompilerParams(vmem_limit_bytes=4 << 20),
        name="add",
    )(in_hbm(kernel.T), arrived, acc)

    place = lax.axis_index("tile")
    from_left = shifted(right, "tile", 1)

    with_low = tile_count > TCOLS
    out_shape = [jax.ShapeDtypeStruct((2, TILE, TILE), f32), jax.ShapeDtypeStruct((2, TILE, ROWS), f32)]
    out_specs = [hbm, vmem]
    if with_low:
        out_shape.append(jax.ShapeDtypeStruct((2, KW, TILE + ROWS), f32))
        out_specs.append(vmem)
    own, first, *low = pl.pallas_call(
        functools.partial(fold_kernel, with_low),
        out_shape=out_shape,
        in_specs=[vmem],
        out_specs=out_specs,
        scratch_shapes=[pltpu.VMEM((2, TILE, TILE - ROWS), f32), pltpu.SemaphoreType.DMA((SIDE,))],
        compiler_params=pltpu.CompilerParams(vmem_limit_bytes=12 << 20),
        cost_estimate=pl.CostEstimate(flops=1 << 22, bytes_accessed=16 << 20, transcendentals=0),
        name="fold",
    )(acc)

    if with_low:
        from_left = jnp.where(place % TCOLS == 0, 0.0, from_left)
    own = pl.pallas_call(
        edge_kernel,
        out_shape=jax.ShapeDtypeStruct((2, TILE, TILE), f32),
        in_specs=[vmem, vmem, hbm],
        out_specs=hbm,
        scratch_shapes=[
            pltpu.VMEM((2, TILE, ROWS), f32),
            pltpu.SemaphoreType.DMA((SIDE // 2,)),
        ],
        input_output_aliases={2: 0},
        compiler_params=pltpu.CompilerParams(vmem_limit_bytes=4 << 20),
        name="edges",
    )(from_left, first, own)
    if with_low:
        (low,) = low
        from_above = shifted(low, "tile", TCOLS)
        from_corner = shifted(low[:, :, TILE:], "tile", TCOLS + 1)
        from_corner = jnp.where(place % TCOLS == 0, 0.0, from_corner)
        own = own.at[:, :KW, :].add(from_above[:, :, :TILE])
        own = own.at[:, :KW, :ROWS].add(from_corner)
    return own.reshape(1, 1, 2, TILE, TILE)


def solution(mesh):
    in_specs = (
        P(("tile", "wp"), None, None),
        P(("tile", "wp"), None),
        P(("tile", "wp"), None),
        P(("tile", "wp"), None),
        P(("tile", "wp"), None),
        P(("tile", "wp")),
        P(),
    )
    out_specs = P("wp", "tile", None, None, None)
    return jax.shard_map(shards, mesh=mesh, in_specs=in_specs, out_specs=out_specs, check_vma=False)
```

profile of v0, /device:TPU:0, one launch (start us, length us, event | category | flops | bytes accessed | tf_op | source)
XLA Modules:
  0.0 59.6 jit_solution(4281726918185707705)
XLA Ops:
  0.0 3.6 %pack.1 = (f32[1568,1,128]{2,1,0:T(1,128)S(1)}, f32[273,144,128]{2,1,0:T(8,128)S(1)}) custom-call(s32[256]{0:T(256)} %bitcast.4, s32[256]{0:T(256)} %patch.1, f32[256,2,128]{2,1,0:T(2,128)} %vis.1, f32[256,128]{1,0:T(8,128)} %weight.1, s32[256,128]{1,0:T(8,128)} %cell.1, s32[256,128]{1,0:T(8,128)} %tap.1), custom_call_target="tpu_custom_call" | custom-call | tf_op jit(solution)/shard_map/pack/pallas_call | solution.py:348
  3.6 28.1 %all_to_all.5.arrived = f32[1568,1,128]{2,1,0:T(1,128)S(1)} all-to-all(f32[1568,1,128]{2,1,0:T(1,128)S(1)} %get-tuple-element.11), channel_id=1, replica_groups=mesh['tile'=8,'wp'=4] {'tile','wp'}, dimensions={0} | all-to-all | bytes 1605632 | tf_op jit(solution)/shard_map/all_to_all | solution.py:369
  31.7 12.5 %add.1 = (f32[273,144,128]{2,1,0:T(8,128)S(1)}, f32[2,8,8,128]{3,2,1,0:T(8,128)S(1)}) custom-call(f32[8,16]{1,0:T(8,128)} %bitcast.3, f32[1568,1,128]{2,1,0:T(1,128)S(1)} %all_to_all.5.arrived, f32[273,144,128]{2,1,0:T(8,128)S(1)} %get-tuple-element.12.acc_in), custom_call_target="tpu_custom_call", output_to_operand_aliasing={{0}: (2, {})} | custom-call | tf_op jit(solution)/shard_map/add/pallas_call | solution.py:371
  44.2 10.7 %collective-permute-start = (f32[2,8,8,128]{3,2,1,0:T(8,128)S(1)}, f32[2,8,8,128]{3,2,1,0:T(8,128)S(1)}, u32[]{:S(2)}, u32[]{:S(2)}) collective-permute-start(f32[2,8,8,128]{3,2,1,0:T(8,128)S(1)} %get-tuple-element.13), channel_id=1, source_target_pairs={{0,4},{4,8},{8,12},{12,16},{16,20},{20,24},{24,28},{1,5},{5,9},{9,... | collective-permute-start | bytes 196616 | tf_op jit(solution)/shard_map/ppermute | solution.py:333
  54.9 3.2 %fold.1 = (f32[2,1024,1024]{2,1,0:T(8,128)}, f32[2,1024,128]{2,1,0:T(8,128)S(1)}) custom-call(f32[273,144,128]{2,1,0:T(8,128)S(1)} %get-tuple-element.14.acc), custom_call_target="tpu_custom_call" | custom-call | flops 4194304 | bytes 16777216 | tf_op jit(solution)/shard_map/fold/pallas_call | solution.py:398
  58.1 0.0 collective-permute-done.edge
  58.1 1.5 %edges.1 = f32[2,1024,1024]{2,1,0:T(8,128)} custom-call(f32[2,8,8,128]{3,2,1,0:T(8,128)S(1)} %collective-permute-done.edge, f32[2,1024,128]{2,1,0:T(8,128)S(1)} %get-tuple-element.15.first, f32[2,1024,1024]{2,1,0:T(8,128)} %get-tuple-element.16.grid_in), custom_call_target="tpu_custom_call", output_to_operand_aliasing={{}: (2, {})} | custom-call | tf_op jit(solution)/shard_map/edges/pallas_call | solution.py:411
Async XLA Ops:
  44.2 13.9 %collective-permute-start = (f32[2,8,8,128]{3,2,1,0:T(8,128)S(1)}, f32[2,8,8,128]{3,2,1,0:T(8,128)S(1)}, u32[]{:S(2)}, u32[]{:S(2)}) collective-permute-start(f32[2,8,8,128]{3,2,1,0:T(8,128)S(1)} %get-tuple-element.13), channel_id=1, source_target_pairs={{0,4},{4,8},{8,12},{12,16},{16,20},{20,24},{24,28},{1,5},{5,9},{9,... | collective-permute-start | bytes 196616 | tf_op jit(solution)/shard_map/ppermute | solution.py:333
where the time goes:
time: 59.5 us; the launch traced here: 59.6 us
  blocking collectives  28.1 us (47%)
  Pallas kernels  20.9 us (35%)
  starting transfers between devices  10.7 us (18%)
    all_to_all x1, blocking collectives, shards(): lax.all_to_all(buckets, ('tile', 'wp'), split_axis=0, concat_axis=0, tile...  28.1 us
    pallas_call x1, Pallas kernels, shards(): pl.pallas_call(functools.partial(add_kernel, peers, cap), out_shape=[pltp...  12.5 us
    ppermute x1, starting transfers between devices, shifted(): return lax.ppermute(block, axis, route)  10.7 us
    pallas_call x1, Pallas kernels, shards(): pl.pallas_call(functools.partial(pack_kernel, peers, cap), out_shape=[jax...  3.62 us
    pallas_call x1, Pallas kernels, shards(): pl.pallas_call(functools.partial(fold_kernel, with_low), out_shape=out_sh...  3.18 us
    pallas_call x1, Pallas kernels, shards(): pl.pallas_call(edge_kernel, out_shape=jax.ShapeDtypeStruct((2, TILE, TILE...  1.54 us
  transfers between devices with their start and end apart: 1, of which 0 were waited for; matrix products, arithmetic and copies ran while one was open for 0% of the time, Pallas kernels for 5%

commit v1 on v0

--- a/solution.py
+++ b/solution.py
@@ -18,7 +18,7 @@
 ROW_BLOCK = 2 * (SUB + KW)
 FIRST = SIDE
 DUMMY = FIRST + PATCHES
-LONG, SHORT = 64, 16
+STEPS = (128, 32, 16)
 
 f32 = jnp.float32
 bf16 = jnp.bfloat16
@@ -29,7 +29,7 @@
 
 
 def pack_kernel(peers, cap, routes, patch, vis, weight, cell, tap, out, acc, *scratch):
-    routes_s, patch_s, vis_v, weight_v, cell_v, tap_v, meta, meta_v, place, sems = scratch
+    routes_s, patch_s, vis_v, weight_v, cell_v, tap_v, count, meta, meta_v, place, sems = scratch
     blocks = vis.shape[0]
     rows = 3 * cap + 1
     sources = (routes, patch, vis, weight, cell, tap)
@@ -46,7 +46,7 @@
             acc[first + i] = jnp.zeros((ROW_BLOCK, ROWS), f32)
 
     def clear(d, carry):
-        meta[d, cap] = 0
+        count[d] = 0
         return carry
 
     def clear_one(i, carry):
@@ -63,13 +63,18 @@
         for i in range(8):
             b = step * 8 + i
             d = routes_s[b]
-            k = meta[d, cap]
-            meta[d, cap] = k + 1
+            k = count[d]
+            count[d] = k + 1
             meta[d, k] = patch_s[b]
             place[b] = d * rows + 3 * k
         return carry
 
+    def put_count(d, carry):
+        meta[d, cap] = count[d]
+        return carry
+
     lax.fori_loop(0, steps, choose, 0)
+    lax.fori_loop(0, peers, put_count, 0, unroll=8)
     meta_copy = pltpu.make_async_copy(meta, meta_v, sems.at[6])
     meta_copy.start()
     for copy in copies[2:]:
@@ -202,7 +207,7 @@
         return total + meta[s, cap]
 
     total = lax.fori_loop(0, peers, gather_source, 0, unroll=2)
-    for k in range(SHORT):
+    for k in range(STEPS[-1]):
         slots[total + k] = DUMMY
 
     def add(first, number):
@@ -215,19 +220,16 @@
             code = jnp.broadcast_to(arrived[row + 2], (8, ROWS)).astype(jnp.int32)
             acc[where_to] += patch_product(re, im, code, entry & 1, table, i % 4 < 2)
 
-    def long_step(step, carry):
-        add(step * LONG, LONG)
-        return carry
-
-    long_steps = total // LONG
-    lax.fori_loop(0, long_steps, long_step, 0)
-    done = long_steps * LONG
-
-    def short_step(step, carry):
-        add(done + step * SHORT, SHORT)
-        return carry
-
-    lax.fori_loop(0, (total - done + SHORT - 1) // SHORT, short_step, 0)
+    done = 0
+    for size in STEPS:
+        steps = (total - done + (size - 1 if size == STEPS[-1] else 0)) // size
+
+        def add_step(step, carry, size=size, done=done):
+            add(done + step * size, size)
+            return carry
+
+        lax.fori_loop(0, steps, add_step, 0)
+        done = done + steps * size
 
     lane = lanes((8, ROWS))
 
@@ -357,6 +359,7 @@
             pltpu.VMEM((blocks, ROWS), f32),
             pltpu.VMEM((blocks, ROWS), jnp.int32),
             pltpu.VMEM((blocks, ROWS), jnp.int32),
+            pltpu.SMEM((peers,), jnp.int32),
             pltpu.SMEM((peers, ROWS), jnp.int32),
             pltpu.VMEM((peers, ROWS), jnp.int32),
             pltpu.SMEM((blocks,), jnp.int32),
@@ -376,7 +379,7 @@
         scratch_shapes=[
             pltpu.VMEM((peers, ROWS), jnp.int32),
             pltpu.SMEM((peers, ROWS), jnp.int32),
-            pltpu.SMEM((peers * cap + max(cap, SHORT),), jnp.int32),
+            pltpu.SMEM((peers * cap + max(cap, STEPS[-1]),), jnp.int32),
             pltpu.SMEM((KW, OVER), f32),
             pltpu.SemaphoreType.DMA,
             pltpu.SemaphoreType.DMA,

time: 59.5 us -> 57 us (0.958)
  the two profiles are of different devices: /device:TPU:0 before, /device:TPU:5 now
where the time goes in v1:
time: 57 us; the launch traced here: 56.4 us
  blocking collectives  26.9 us (47%)
  Pallas kernels  15.2 us (27%)
  starting transfers between devices  14.3 us (25%)
    all_to_all x1, blocking collectives, shards(): lax.all_to_all(buckets, ('tile', 'wp'), split_axis=0, concat_axis=0, tile...  26.9 us
    ppermute x1, starting transfers between devices, shifted(): return lax.ppermute(block, axis, route)  14.3 us
    pallas_call x1, Pallas kernels, shards(): pl.pallas_call(functools.partial(add_kernel, peers, cap), out_shape=[pltp...  7.19 us
    pallas_call x1, Pallas kernels, shards(): pl.pallas_call(functools.partial(pack_kernel, peers, cap), out_shape=[jax...  3.32 us
    pallas_call x1, Pallas kernels, shards(): pl.pallas_call(functools.partial(fold_kernel, with_low), out_shape=out_sh...  3.18 us
    pallas_call x1, Pallas kernels, shards(): pl.pallas_call(edge_kernel, out_shape=jax.ShapeDtypeStruct((2, TILE, TILE...  1.54 us
  transfers between devices with their start and end apart: 1, of which 0 were waited for; matrix products, arithmetic and copies ran while one was open for 0% of the time, Pallas kernels for 6%

profile of v1, /device:TPU:5, one launch (start us, length us, event | category | flops | bytes accessed | tf_op | source)
XLA Modules:
  0.0 56.4 jit_solution(10004748720707488322)
XLA Ops:
  0.0 3.3 %pack.1 = (f32[1568,1,128]{2,1,0:T(1,128)S(1)}, f32[273,144,128]{2,1,0:T(8,128)S(1)}) custom-call(s32[256]{0:T(256)} %bitcast.4, s32[256]{0:T(256)} %patch.1, f32[256,2,128]{2,1,0:T(2,128)} %vis.1, f32[256,128]{1,0:T(8,128)} %weight.1, s32[256,128]{1,0:T(8,128)} %cell.1, s32[256,128]{1,0:T(8,128)} %tap.1), custom_call_target="tpu_custom_call" | custom-call | tf_op jit(solution)/shard_map/pack/pallas_call | solution.py:350
  3.3 26.9 %all_to_all.5.arrived = f32[1568,1,128]{2,1,0:T(1,128)S(1)} all-to-all(f32[1568,1,128]{2,1,0:T(1,128)S(1)} %get-tuple-element.11), channel_id=1, replica_groups=mesh['tile'=8,'wp'=4] {'tile','wp'}, dimensions={0} | all-to-all | bytes 1605632 | tf_op jit(solution)/shard_map/all_to_all | solution.py:372
  30.2 7.2 %add.1 = (f32[273,144,128]{2,1,0:T(8,128)S(1)}, f32[2,8,8,128]{3,2,1,0:T(8,128)S(1)}) custom-call(f32[8,16]{1,0:T(8,128)} %bitcast.3, f32[1568,1,128]{2,1,0:T(1,128)S(1)} %all_to_all.5.arrived, f32[273,144,128]{2,1,0:T(8,128)S(1)} %get-tuple-element.12.acc_in), custom_call_target="tpu_custom_call", output_to_operand_aliasing={{0}: (2, {})} | custom-call | tf_op jit(solution)/shard_map/add/pallas_call | solution.py:374
  37.4 14.3 %collective-permute-start = (f32[2,8,8,128]{3,2,1,0:T(8,128)S(1)}, f32[2,8,8,128]{3,2,1,0:T(8,128)S(1)}, u32[]{:S(2)}, u32[]{:S(2)}) collective-permute-start(f32[2,8,8,128]{3,2,1,0:T(8,128)S(1)} %get-tuple-element.13), channel_id=1, source_target_pairs={{0,4},{4,8},{8,12},{12,16},{16,20},{20,24},{24,28},{1,5},{5,9},{9,... | collective-permute-start | bytes 196616 | tf_op jit(solution)/shard_map/ppermute | solution.py:335
  51.7 3.2 %fold.1 = (f32[2,1024,1024]{2,1,0:T(8,128)}, f32[2,1024,128]{2,1,0:T(8,128)S(1)}) custom-call(f32[273,144,128]{2,1,0:T(8,128)S(1)} %get-tuple-element.14.acc), custom_call_target="tpu_custom_call" | custom-call | flops 4194304 | bytes 16777216 | tf_op jit(solution)/shard_map/fold/pallas_call | solution.py:401
  54.9 0.0 collective-permute-done.edge
  54.9 1.5 %edges.1 = f32[2,1024,1024]{2,1,0:T(8,128)} custom-call(f32[2,8,8,128]{3,2,1,0:T(8,128)S(1)} %collective-permute-done.edge, f32[2,1024,128]{2,1,0:T(8,128)S(1)} %get-tuple-element.15.first, f32[2,1024,1024]{2,1,0:T(8,128)} %get-tuple-element.16.grid_in), custom_call_target="tpu_custom_call", output_to_operand_aliasing={{}: (2, {})} | custom-call | tf_op jit(solution)/shard_map/edges/pallas_call | solution.py:414
Async XLA Ops:
  37.4 17.5 %collective-permute-start = (f32[2,8,8,128]{3,2,1,0:T(8,128)S(1)}, f32[2,8,8,128]{3,2,1,0:T(8,128)S(1)}, u32[]{:S(2)}, u32[]{:S(2)}) collective-permute-start(f32[2,8,8,128]{3,2,1,0:T(8,128)S(1)} %get-tuple-element.13), channel_id=1, source_target_pairs={{0,4},{4,8},{8,12},{12,16},{16,20},{20,24},{24,28},{1,5},{5,9},{9,... | collective-permute-start | bytes 196616 | tf_op jit(solution)/shard_map/ppermute | solution.py:335

commit v2 on v1

--- a/solution.py
+++ b/solution.py
@@ -18,7 +18,7 @@
 ROW_BLOCK = 2 * (SUB + KW)
 FIRST = SIDE
 DUMMY = FIRST + PATCHES
-STEPS = (128, 32, 16)
+STEPS = (128, 64, 32, 16)
 
 f32 = jnp.float32
 bf16 = jnp.bfloat16
@@ -98,7 +98,7 @@
             out[row + 2] = code[i : i + 1, :]
         return carry
 
-    lax.fori_loop(0, steps, move, 0)
+    lax.fori_loop(0, steps, move, 0, unroll=4)
     meta_copy.wait()
 
     def put_meta(d, carry):
@@ -281,7 +281,7 @@
         copy_out(band).start()
         return carry
 
-    lax.fori_loop(0, SIDE, fold, 0)
+    lax.fori_loop(0, SIDE, fold, 0, unroll=2)
     if with_low:
         for c in range(2):
             before = jnp.zeros((8, ROWS), f32)
@@ -320,7 +320,7 @@
         put(pair).start()
         return carry
 
-    lax.fori_loop(0, pairs, add, 0)
+    lax.fori_loop(0, pairs, add, 0, unroll=4)
     for pair in range(pairs):
         put(pair).wait()
 

time: 57 us -> 57 us (level)
  the two profiles are of different devices: /device:TPU:5 before, /device:TPU:4 now
where the time goes in v2:
time: 57 us; the launch traced here: 56.8 us
  blocking collectives  26.6 us (47%)
  Pallas kernels  18.1 us (32%)
  starting transfers between devices  12 us (21%)
    all_to_all x1, blocking collectives, shards(): lax.all_to_all(buckets, ('tile', 'wp'), split_axis=0, concat_axis=0, tile...  26.6 us
    ppermute x1, starting transfers between devices, shifted(): return lax.ppermute(block, axis, route)  12 us
    pallas_call x1, Pallas kernels, shards(): pl.pallas_call(functools.partial(add_kernel, peers, cap), out_shape=[pltp...  10.1 us
    pallas_call x1, Pallas kernels, shards(): pl.pallas_call(functools.partial(pack_kernel, peers, cap), out_shape=[jax...  3.32 us
    pallas_call x1, Pallas kernels, shards(): pl.pallas_call(functools.partial(fold_kernel, with_low), out_shape=out_sh...  3.18 us
    pallas_call x1, Pallas kernels, shards(): pl.pallas_call(edge_kernel, out_shape=jax.ShapeDtypeStruct((2, TILE, TILE...  1.53 us
  transfers between devices with their start and end apart: 1, of which 0 were waited for; matrix products, arithmetic and copies ran while one was open for 0% of the time, Pallas kernels for 6%

profile of v2, /device:TPU:4, one launch (start us, length us, event | category | flops | bytes accessed | tf_op | source)
XLA Modules:
  0.0 56.8 jit_solution(13484795209289723970)
XLA Ops:
  0.0 3.3 %pack.1 = (f32[1568,1,128]{2,1,0:T(1,128)S(1)}, f32[273,144,128]{2,1,0:T(8,128)S(1)}) custom-call(s32[256]{0:T(256)} %bitcast.4, s32[256]{0:T(256)} %patch.1, f32[256,2,128]{2,1,0:T(2,128)} %vis.1, f32[256,128]{1,0:T(8,128)} %weight.1, s32[256,128]{1,0:T(8,128)} %cell.1, s32[256,128]{1,0:T(8,128)} %tap.1), custom_call_target="tpu_custom_call" | custom-call | tf_op jit(solution)/shard_map/pack/pallas_call | solution.py:350
  3.3 26.6 %all_to_all.5.arrived = f32[1568,1,128]{2,1,0:T(1,128)S(1)} all-to-all(f32[1568,1,128]{2,1,0:T(1,128)S(1)} %get-tuple-element.11), channel_id=1, replica_groups=mesh['tile'=8,'wp'=4] {'tile','wp'}, dimensions={0} | all-to-all | bytes 1605632 | tf_op jit(solution)/shard_map/all_to_all | solution.py:372
  29.9 10.1 %add.1 = (f32[273,144,128]{2,1,0:T(8,128)S(1)}, f32[2,8,8,128]{3,2,1,0:T(8,128)S(1)}) custom-call(f32[8,16]{1,0:T(8,128)} %bitcast.3, f32[1568,1,128]{2,1,0:T(1,128)S(1)} %all_to_all.5.arrived, f32[273,144,128]{2,1,0:T(8,128)S(1)} %get-tuple-element.12.acc_in), custom_call_target="tpu_custom_call", output_to_operand_aliasing={{0}: (2, {})} | custom-call | tf_op jit(solution)/shard_map/add/pallas_call | solution.py:374
  40.0 12.0 %collective-permute-start = (f32[2,8,8,128]{3,2,1,0:T(8,128)S(1)}, f32[2,8,8,128]{3,2,1,0:T(8,128)S(1)}, u32[]{:S(2)}, u32[]{:S(2)}) collective-permute-start(f32[2,8,8,128]{3,2,1,0:T(8,128)S(1)} %get-tuple-element.13), channel_id=1, source_target_pairs={{0,4},{4,8},{8,12},{12,16},{16,20},{20,24},{24,28},{1,5},{5,9},{9,... | collective-permute-start | bytes 196616 | tf_op jit(solution)/shard_map/ppermute | solution.py:335
  52.0 3.2 %fold.1 = (f32[2,1024,1024]{2,1,0:T(8,128)}, f32[2,1024,128]{2,1,0:T(8,128)S(1)}) custom-call(f32[273,144,128]{2,1,0:T(8,128)S(1)} %get-tuple-element.14.acc), custom_call_target="tpu_custom_call" | custom-call | flops 4194304 | bytes 16777216 | tf_op jit(solution)/shard_map/fold/pallas_call | solution.py:401
  55.2 0.0 collective-permute-done.edge
  55.2 1.5 %edges.1 = f32[2,1024,1024]{2,1,0:T(8,128)} custom-call(f32[2,8,8,128]{3,2,1,0:T(8,128)S(1)} %collective-permute-done.edge, f32[2,1024,128]{2,1,0:T(8,128)S(1)} %get-tuple-element.15.first, f32[2,1024,1024]{2,1,0:T(8,128)} %get-tuple-element.16.grid_in), custom_call_target="tpu_custom_call", output_to_operand_aliasing={{}: (2, {})} | custom-call | tf_op jit(solution)/shard_map/edges/pallas_call | solution.py:414
Async XLA Ops:
  40.0 15.2 %collective-permute-start = (f32[2,8,8,128]{3,2,1,0:T(8,128)S(1)}, f32[2,8,8,128]{3,2,1,0:T(8,128)S(1)}, u32[]{:S(2)}, u32[]{:S(2)}) collective-permute-start(f32[2,8,8,128]{3,2,1,0:T(8,128)S(1)} %get-tuple-element.13), channel_id=1, source_target_pairs={{0,4},{4,8},{8,12},{12,16},{16,20},{20,24},{24,28},{1,5},{5,9},{9,... | collective-permute-start | bytes 196616 | tf_op jit(solution)/shard_map/ppermute | solution.py:335

commit v3 on v2

--- a/solution.py
+++ b/solution.py
@@ -218,7 +218,7 @@
             re = jnp.broadcast_to(arrived[row], (8, ROWS))
             im = jnp.broadcast_to(arrived[row + 1], (8, ROWS))
             code = jnp.broadcast_to(arrived[row + 2], (8, ROWS)).astype(jnp.int32)
-            acc[where_to] += patch_product(re, im, code, entry & 1, table, i % 4 < 2)
+            acc[where_to] += patch_product(re, im, code, entry & 1, table, i % 4 < 2 and i % 16 != 13)
 
     done = 0
     for size in STEPS:

time: 57 us -> 57.4 us (level)
  the two profiles are of different devices: /device:TPU:4 before, /device:TPU:7 now
where the time goes in v3:
time: 57.4 us; the launch traced here: 57.1 us
  blocking collectives  26.3 us (46%)
  Pallas kernels  15.5 us (27%)
  starting transfers between devices  15.2 us (26%)
    all_to_all x1, blocking collectives, shards(): lax.all_to_all(buckets, ('tile', 'wp'), split_axis=0, concat_axis=0, tile...  26.3 us
    ppermute x1, starting transfers between devices, shifted(): return lax.ppermute(block, axis, route)  15.2 us
    pallas_call x1, Pallas kernels, shards(): pl.pallas_call(functools.partial(add_kernel, peers, cap), out_shape=[pltp...  7.45 us
    pallas_call x1, Pallas kernels, shards(): pl.pallas_call(functools.partial(pack_kernel, peers, cap), out_shape=[jax...  3.32 us
    pallas_call x1, Pallas kernels, shards(): pl.pallas_call(functools.partial(fold_kernel, with_low), out_shape=out_sh...  3.18 us
    pallas_call x1, Pallas kernels, shards(): pl.pallas_call(edge_kernel, out_shape=jax.ShapeDtypeStruct((2, TILE, TILE...  1.53 us
  transfers between devices with their start and end apart: 1, of which 0 were waited for; matrix products, arithmetic and copies ran while one was open for 0% of the time, Pallas kernels for 6%

profile of v3, /device:TPU:7, one launch (start us, length us, event | category | flops | bytes accessed | tf_op | source)
XLA Modules:
  0.0 57.1 jit_solution(5905005863711390218)
XLA Ops:
  0.0 3.3 %pack.1 = (f32[1568,1,128]{2,1,0:T(1,128)S(1)}, f32[273,144,128]{2,1,0:T(8,128)S(1)}) custom-call(s32[256]{0:T(256)} %bitcast.4, s32[256]{0:T(256)} %patch.1, f32[256,2,128]{2,1,0:T(2,128)} %vis.1, f32[256,128]{1,0:T(8,128)} %weight.1, s32[256,128]{1,0:T(8,128)} %cell.1, s32[256,128]{1,0:T(8,128)} %tap.1), custom_call_target="tpu_custom_call" | custom-call | tf_op jit(solution)/shard_map/pack/pallas_call | solution.py:350
  3.3 26.3 %all_to_all.5.arrived = f32[1568,1,128]{2,1,0:T(1,128)S(1)} all-to-all(f32[1568,1,128]{2,1,0:T(1,128)S(1)} %get-tuple-element.11), channel_id=1, replica_groups=mesh['tile'=8,'wp'=4] {'tile','wp'}, dimensions={0} | all-to-all | bytes 1605632 | tf_op jit(solution)/shard_map/all_to_all | solution.py:372
  29.6 7.5 %add.1 = (f32[273,144,128]{2,1,0:T(8,128)S(1)}, f32[2,8,8,128]{3,2,1,0:T(8,128)S(1)}) custom-call(f32[8,16]{1,0:T(8,128)} %bitcast.3, f32[1568,1,128]{2,1,0:T(1,128)S(1)} %all_to_all.5.arrived, f32[273,144,128]{2,1,0:T(8,128)S(1)} %get-tuple-element.12.acc_in), custom_call_target="tpu_custom_call", output_to_operand_aliasing={{0}: (2, {})} | custom-call | tf_op jit(solution)/shard_map/add/pallas_call | solution.py:374
  37.1 15.2 %collective-permute-start = (f32[2,8,8,128]{3,2,1,0:T(8,128)S(1)}, f32[2,8,8,128]{3,2,1,0:T(8,128)S(1)}, u32[]{:S(2)}, u32[]{:S(2)}) collective-permute-start(f32[2,8,8,128]{3,2,1,0:T(8,128)S(1)} %get-tuple-element.13), channel_id=1, source_target_pairs={{0,4},{4,8},{8,12},{12,16},{16,20},{20,24},{24,28},{1,5},{5,9},{9,... | collective-permute-start | bytes 196616 | tf_op jit(solution)/shard_map/ppermute | solution.py:335
  52.3 3.2 %fold.1 = (f32[2,1024,1024]{2,1,0:T(8,128)}, f32[2,1024,128]{2,1,0:T(8,128)S(1)}) custom-call(f32[273,144,128]{2,1,0:T(8,128)S(1)} %get-tuple-element.14.acc), custom_call_target="tpu_custom_call" | custom-call | flops 4194304 | bytes 16777216 | tf_op jit(solution)/shard_map/fold/pallas_call | solution.py:401
  55.5 0.0 collective-permute-done.edge
  55.5 1.5 %edges.1 = f32[2,1024,1024]{2,1,0:T(8,128)} custom-call(f32[2,8,8,128]{3,2,1,0:T(8,128)S(1)} %collective-permute-done.edge, f32[2,1024,128]{2,1,0:T(8,128)S(1)} %get-tuple-element.15.first, f32[2,1024,1024]{2,1,0:T(8,128)} %get-tuple-element.16.grid_in), custom_call_target="tpu_custom_call", output_to_operand_aliasing={{}: (2, {})} | custom-call | tf_op jit(solution)/shard_map/edges/pallas_call | solution.py:414
Async XLA Ops:
  37.1 18.4 %collective-permute-start = (f32[2,8,8,128]{3,2,1,0:T(8,128)S(1)}, f32[2,8,8,128]{3,2,1,0:T(8,128)S(1)}, u32[]{:S(2)}, u32[]{:S(2)}) collective-permute-start(f32[2,8,8,128]{3,2,1,0:T(8,128)S(1)} %get-tuple-element.13), channel_id=1, source_target_pairs={{0,4},{4,8},{8,12},{12,16},{16,20},{20,24},{24,28},{1,5},{5,9},{9,... | collective-permute-start | bytes 196616 | tf_op jit(solution)/shard_map/ppermute | solution.py:335
